TPU v7x, 32 devices: a whole 2x2x4 slice. The times are simulated.
32 devices in a mesh: horiz: 8 (over z, y), vert: 4 (over x, core).
Axes of the slice: x: 2, y: 2, z: 4, core: 2. Of those that a mesh axis runs over, the one named last changes fastest.
Arguments:
- tracer: bfloat16 [8, 2048, 128], P('vert', 'horiz'), may hold values from -6 to 6
- explicit_tiles: bfloat16 [8, 16, 7, 128, 128], P('vert', 'horiz'), may hold values from -0.25 to 0.25
- tile_columns: int32 [8, 16, 7], P('vert', 'horiz'), may hold values from 0 to 127, as said below
- tile_counts: int32 [8, 16], P('vert', 'horiz'), may hold values from 4 to 7
- surface_source: bfloat16 [2048, 128], P('horiz'), may hold values from -6 to 6
- implicit_columns: float32 [2048, 8, 8], P(('horiz', 'vert')), may hold values from -0.53033009 to 1
- settling: float32 [128], replicated, may hold values from 0.02 to 0.5
- wet_mask: int32 [8, 2048], P('vert', 'horiz'), may hold values 0 or 1
Outputs:
- tracer_out: bfloat16 [8, 2048, 128], P('vert', 'horiz')
Inputs may be any that keep to these rules, and one draw needn't show every extreme that they name: `tile_columns`: slot 0 of block row (l, t) names the row's own tile l * 16 + t; the other slots name distinct tiles within 2 levels and 2 tiles of it, inside the grid.
All inputs are finite; a program needn't handle non-finite values. No bound on the sum of `wet_mask` on one device may be relied on, other than what follows from the above.
Results may differ from a plain program's by a relative error of at most 0.015.
Values may be sent and summed in bfloat16 or wider, within the bound.
A program may use at most 64 MiB of HBM per device.

v0:
```python
import jax
import jax.numpy as jnp
from jax import lax
from jax.sharding import PartitionSpec as P

REACH = 2
STEPS = 4


def extended(shard, sides, width):
    for axis, dim in sides:
        size, length = (lax.axis_size(axis), shard.shape[dim])
        up = [(i, (i + 1) % size) for i in range(size - 1)]
        down = [(j, i) for i, j in up]
        last = lax.slice_in_dim(shard, length - width, length, axis=dim)
        leading = lax.slice_in_dim(shard, 0, width, axis=dim)
        before = lax.ppermute(last, axis, up)
        after = lax.ppermute(leading, axis, down)
        shard = jnp.concatenate([before, shard, after], axis=dim)
    return shard


def from_behind(value, axis, steps):
    count = lax.axis_size(axis)
    leading, last = (max(0, -steps), min(count, count - steps))
    return lax.ppermute(value, axis, [(source, source + steps) for source in range(leading, last)])


def on_device(
    tracer,
    explicit_tiles,
    tile_columns,
    tile_counts,
    surface_source,
    implicit_columns,
    settling,
    wet_mask,
):
    lev_dev, cells_dev, classes = tracer.shape
    tile_size = explicit_tiles.shape[-1]
    tiles_dev = cells_dev // tile_size
    slot_count = explicit_tiles.shape[2]
    h_tiles = tiles_dev * lax.axis_size("horiz")
    wide_tiles = tiles_dev + 2 * REACH
    first_level = lax.axis_index("vert") * lev_dev
    first_tile = lax.axis_index("horiz") * tiles_dev
    col_level = tile_columns // h_tiles - (first_level - REACH)
    col_tile = tile_columns % h_tiles - (first_tile - REACH)
    position = col_level * wide_tiles + col_tile
    live_slots = (
        jnp.arange(slot_count, dtype=jnp.int32)[None, None, :] < tile_counts[:, :, None]
    ).astype(jnp.bfloat16)
    on_top = first_level + jnp.arange(lev_dev, dtype=jnp.int32) == 0
    source = surface_source.astype(jnp.float32)
    fall_rate = settling[None, None, :]
    wet_cells = wet_mask.astype(jnp.bfloat16)[:, :, None]
    all_columns = lax.all_gather(implicit_columns, "vert", axis=0, tiled=True)
    own_rows = lax.dynamic_slice_in_dim(all_columns, first_level, lev_dev, 1)
    current = tracer
    for step_index in range(STEPS):
        slab_grid = current.reshape(lev_dev, tiles_dev, tile_size, classes)
        padded = extended(slab_grid, (("horiz", 1), ("vert", 0)), REACH)
        flattened = padded.reshape(-1, tile_size, classes)
        picked = flattened[position] * live_slots[:, :, :, None, None]
        explicit_flow = jnp.einsum(
            "ltjab,ltjbs->ltas", explicit_tiles, picked, preferred_element_type=jnp.float32
        )
        explicit_flow = explicit_flow.reshape(lev_dev, cells_dev, classes)
        explicit_flow = explicit_flow + jnp.where(on_top[:, None, None], source[None, :, :], 0.0)
        loaded = explicit_flow.astype(jnp.bfloat16)
        mixed_col = jnp.einsum(
            "ckm,mcs->kcs",
            own_rows,
            lax.all_gather(loaded, "vert", axis=0, tiled=True).astype(jnp.float32),
            precision=lax.Precision.HIGHEST,
        )
        upper_level = from_behind(mixed_col[-1].astype(jnp.bfloat16), "vert", 1).astype(jnp.float32)
        from_above = jnp.concatenate([upper_level[None], mixed_col[:-1]], axis=0)
        settled = (1.0 - fall_rate) * mixed_col + fall_rate * from_above
        current = (settled * wet_cells.astype(jnp.float32)).astype(jnp.bfloat16)
    return current


def solution(mesh):
    placed = (
        P("vert", "horiz", None),
        P("vert", "horiz", None, None, None),
        P("vert", "horiz", None),
        P("vert", "horiz"),
        P("horiz", None),
        P(("horiz", "vert"), None, None),
        P(),
        P("vert", "horiz"),
    )
    return jax.shard_map(
        on_device, mesh=mesh, in_specs=placed, out_specs=P("vert", "horiz", None), check_vma=False
    )
```

profile of v0, /device:TPU:1, one launch (start us, length us, event | category | flops | bytes accessed | tf_op | source)
XLA Modules:
  0.0 167.6 jit_solution(6005104641196930024)
XLA Ops:
  0.0 1.4 collective-permute-start.1
  1.4 4.6 %collective-permute-start = (bf16[2,2,128,128]{3,2,1,0:T(8,128)(2,1)}, bf16[2,2,128,128]{3,2,1,0:T(8,128)(2,1)S(1)}, u32[]{:S(2)}, u32[]{:S(2)}) collective-permute-start(bf16[2,2,128,128]{3,2,1,0:T(8,128)(2,1)} %bitcast.83), channel_id=1, source_target_pairs={{0,4},{4,8},{8,12},{12,16},{16,20},{20,24},{24,28},{1,5},{5,9},{9,... | collective-permute-start | bytes 393224 | tf_op jit(solution)/shard_map/ppermute | solution.py:17
  8.7 11.3 %all_gather.16 = f32[256,8,8]{2,1,0:T(8,128)S(1)} all-gather(f32[64,8,8]{2,1,0:T(8,128)S(1)} %copy.38), channel_id=1, replica_groups=mesh['horiz'=8,'vert'=4] {'vert'}, dimensions={0}, use_global_device_ids=true | all-gather | bytes 81920 | tf_op jit(solution)/shard_map/all_gather | solution.py:57
  20.1 2.1 %collective-permute-start.3 = (bf16[2,6,128,128]{3,2,1,0:T(8,128)(2,1)S(1)}, bf16[2,6,128,128]{3,2,1,0:T(8,128)(2,1)S(1)}, u32[]{:S(2)}, u32[]{:S(2)}) collective-permute-start(bf16[2,6,128,128]{3,2,1,0:T(8,128)(2,1)S(1)} %pad_maximum_fusion.4), channel_id=1, source_target_pairs={{1,0},{2,1},{3,2},{5,4},{6,5},{7,6},{9,8},{10,9},{11,10},{13,12},{... | collective-permute-start | bytes 1179656 | tf_op jit(solution)/shard_map/ppermute | solution.py:18
  22.1 3.5 %collective-permute-start.2 = (bf16[2,6,128,128]{3,2,1,0:T(8,128)(2,1)S(1)}, bf16[2,6,128,128]{3,2,1,0:T(8,128)(2,1)S(1)}, u32[]{:S(2)}, u32[]{:S(2)}) collective-permute-start(bf16[2,6,128,128]{3,2,1,0:T(8,128)(2,1)S(1)} %pad_maximum_fusion.4), channel_id=1, source_target_pairs={{0,1},{1,2},{2,3},{4,5},{5,6},{6,7},{8,9},{9,10},{10,11},{12,13},{... | collective-permute-start | bytes 1179656 | tf_op jit(solution)/shard_map/ppermute | solution.py:17
  25.7 3.4 %collective-permute-done.3 = bf16[2,6,128,128]{3,2,1,0:T(8,128)(2,1)S(1)} collective-permute-done((bf16[2,6,128,128]{3,2,1,0:T(8,128)(2,1)S(1)}, bf16[2,6,128,128]{3,2,1,0:T(8,128)(2,1)S(1)}, u32[]{:S(2)}, u32[]{:S(2)}) %collective-permute-start.3) | collective-permute-done | bytes 393248 | tf_op jit(solution)/shard_map/ppermute | solution.py:18
  31.4 1.6 gather_fusion
  33.0 1.7 fusion.6
  34.8 8.4 %all_gather.15 = bf16[8,256,128]{2,1,0:T(8,128)(2,1)S(1)} all-gather(bf16[2,256,128]{2,1,0:T(8,128)(2,1)S(1)} %fusion.16), channel_id=1, replica_groups=mesh['horiz'=8,'vert'=4] {'vert'}, dimensions={0}, use_global_device_ids=true | all-gather | bytes 655360 | tf_op jit(solution)/shard_map/all_gather | solution.py:74
  44.6 2.5 %collective-permute-start.4 = (bf16[256,128]{1,0:T(8,128)(2,1)S(1)}, bf16[256,128]{1,0:T(8,128)(2,1)S(1)}, u32[]{:S(2)}, u32[]{:S(2)}) collective-permute-start(bf16[256,128]{1,0:T(8,128)(2,1)S(1)} %bitcast.90), channel_id=1, source_target_pairs={{0,1},{1,2},{2,3},{4,5},{5,6},{6,7},{8,9},{9,10},{10,11},{12,13},{... | collective-permute-start | bytes 196616 | tf_op jit(solution)/shard_map/ppermute | solution.py:26
  48.8 4.0 %collective-permute-start.5 = (bf16[2,2,128,128]{3,2,1,0:T(8,128)(2,1)S(1)}, bf16[2,2,128,128]{3,2,1,0:T(8,128)(2,1)S(1)}, u32[]{:S(2)}, u32[]{:S(2)}) collective-permute-start(bf16[2,2,128,128]{3,2,1,0:T(8,128)(2,1)S(1)} %copy.42), channel_id=1, source_target_pairs={{0,4},{4,8},{8,12},{12,16},{16,20},{20,24},{24,28},{1,5},{5,9},{9,... | collective-permute-start | bytes 393224 | tf_op jit(solution)/shard_map/ppermute | solution.py:17
  52.9 1.3 collective-permute-start.6
  54.2 2.0 %collective-permute-done.5 = bf16[2,2,128,128]{3,2,1,0:T(8,128)(2,1)S(1)} collective-permute-done((bf16[2,2,128,128]{3,2,1,0:T(8,128)(2,1)S(1)}, bf16[2,2,128,128]{3,2,1,0:T(8,128)(2,1)S(1)}, u32[]{:S(2)}, u32[]{:S(2)}) %collective-permute-start.5) | collective-permute-done | bytes 131104 | tf_op jit(solution)/shard_map/ppermute | solution.py:17
  56.2 3.8 %collective-permute-done.6 = bf16[2,2,128,128]{3,2,1,0:T(8,128)(2,1)S(1)} collective-permute-done((bf16[2,2,128,128]{3,2,1,0:T(8,128)(2,1)S(1)}, bf16[2,2,128,128]{3,2,1,0:T(8,128)(2,1)S(1)}, u32[]{:S(2)}, u32[]{:S(2)}) %collective-permute-start.6) | collective-permute-done | bytes 131104 | tf_op jit(solution)/shard_map/ppermute | solution.py:18
  60.1 2.5 %collective-permute-start.8 = (bf16[2,6,128,128]{3,2,1,0:T(8,128)(2,1)S(1)}, bf16[2,6,128,128]{3,2,1,0:T(8,128)(2,1)S(1)}, u32[]{:S(2)}, u32[]{:S(2)}) collective-permute-start(bf16[2,6,128,128]{3,2,1,0:T(8,128)(2,1)S(1)} %constant_dynamic-update-slice_fusion), channel_id=1, source_target_pairs={{1,0},{2,1},{3,2},{5,4},{6,5},{7,6},{9,8},{10,9},{11,10},{13,12},{... | collective-permute-start | bytes 1179656 | tf_op jit(solution)/shard_map/ppermute | solution.py:18
  62.6 3.6 %collective-permute-start.7 = (bf16[2,6,128,128]{3,2,1,0:T(8,128)(2,1)S(1)}, bf16[2,6,128,128]{3,2,1,0:T(8,128)(2,1)S(1)}, u32[]{:S(2)}, u32[]{:S(2)}) collective-permute-start(bf16[2,6,128,128]{3,2,1,0:T(8,128)(2,1)S(1)} %constant_dynamic-update-slice_fusion), channel_id=1, source_target_pairs={{0,1},{1,2},{2,3},{4,5},{5,6},{6,7},{8,9},{9,10},{10,11},{12,13},{... | collective-permute-start | bytes 1179656 | tf_op jit(solution)/shard_map/ppermute | solution.py:17
  66.2 3.5 %collective-permute-done.8 = bf16[2,6,128,128]{3,2,1,0:T(8,128)(2,1)S(1)} collective-permute-done((bf16[2,6,128,128]{3,2,1,0:T(8,128)(2,1)S(1)}, bf16[2,6,128,128]{3,2,1,0:T(8,128)(2,1)S(1)}, u32[]{:S(2)}, u32[]{:S(2)}) %collective-permute-start.8) | collective-permute-done | bytes 393248 | tf_op jit(solution)/shard_map/ppermute | solution.py:18
  71.1 1.6 gather_fusion.1
  72.7 1.6 fusion.4
  74.5 8.4 %all_gather.17 = bf16[8,256,128]{2,1,0:T(8,128)(2,1)S(1)} all-gather(bf16[2,256,128]{2,1,0:T(8,128)(2,1)S(1)} %fusion.17), channel_id=1, replica_groups=mesh['horiz'=8,'vert'=4] {'vert'}, dimensions={0}, use_global_device_ids=true | all-gather | bytes 655360 | tf_op jit(solution)/shard_map/all_gather | solution.py:74
  84.2 2.5 %collective-permute-start.9 = (bf16[256,128]{1,0:T(8,128)(2,1)S(1)}, bf16[256,128]{1,0:T(8,128)(2,1)S(1)}, u32[]{:S(2)}, u32[]{:S(2)}) collective-permute-start(bf16[256,128]{1,0:T(8,128)(2,1)S(1)} %bitcast.91), channel_id=1, source_target_pairs={{0,1},{1,2},{2,3},{4,5},{5,6},{6,7},{8,9},{9,10},{10,11},{12,13},{... | collective-permute-start | bytes 196616 | tf_op jit(solution)/shard_map/ppermute | solution.py:26
  86.8 1.2 collective-permute-done.9
  88.5 3.1 %collective-permute-start.10 = (bf16[2,2,128,128]{3,2,1,0:T(8,128)(2,1)S(1)}, bf16[2,2,128,128]{3,2,1,0:T(8,128)(2,1)S(1)}, u32[]{:S(2)}, u32[]{:S(2)}) collective-permute-start(bf16[2,2,128,128]{3,2,1,0:T(8,128)(2,1)S(1)} %copy.47), channel_id=1, source_target_pairs={{0,4},{4,8},{8,12},{12,16},{16,20},{20,24},{24,28},{1,5},{5,9},{9,... | collective-permute-start | bytes 393224 | tf_op jit(solution)/shard_map/ppermute | solution.py:17
  91.6 1.3 collective-permute-start.11
  92.9 2.0 %collective-permute-done.10 = bf16[2,2,128,128]{3,2,1,0:T(8,128)(2,1)S(1)} collective-permute-done((bf16[2,2,128,128]{3,2,1,0:T(8,128)(2,1)S(1)}, bf16[2,2,128,128]{3,2,1,0:T(8,128)(2,1)S(1)}, u32[]{:S(2)}, u32[]{:S(2)}) %collective-permute-start.10) | collective-permute-done | bytes 131104 | tf_op jit(solution)/shard_map/ppermute | solution.py:17
  95.0 3.8 %collective-permute-done.11 = bf16[2,2,128,128]{3,2,1,0:T(8,128)(2,1)S(1)} collective-permute-done((bf16[2,2,128,128]{3,2,1,0:T(8,128)(2,1)S(1)}, bf16[2,2,128,128]{3,2,1,0:T(8,128)(2,1)S(1)}, u32[]{:S(2)}, u32[]{:S(2)}) %collective-permute-start.11) | collective-permute-done | bytes 131104 | tf_op jit(solution)/shard_map/ppermute | solution.py:18
  98.8 2.5 %collective-permute-start.13 = (bf16[2,6,128,128]{3,2,1,0:T(8,128)(2,1)S(1)}, bf16[2,6,128,128]{3,2,1,0:T(8,128)(2,1)S(1)}, u32[]{:S(2)}, u32[]{:S(2)}) collective-permute-start(bf16[2,6,128,128]{3,2,1,0:T(8,128)(2,1)S(1)} %constant_dynamic-update-slice_fusion.3), channel_id=1, source_target_pairs={{1,0},{2,1},{3,2},{5,4},{6,5},{7,6},{9,8},{10,9},{11,10},{13,12},{... | collective-permute-start | bytes 1179656 | tf_op jit(solution)/shard_map/ppermute | solution.py:18
  101.4 3.6 %collective-permute-start.12 = (bf16[2,6,128,128]{3,2,1,0:T(8,128)(2,1)S(1)}, bf16[2,6,128,128]{3,2,1,0:T(8,128)(2,1)S(1)}, u32[]{:S(2)}, u32[]{:S(2)}) collective-permute-start(bf16[2,6,128,128]{3,2,1,0:T(8,128)(2,1)S(1)} %constant_dynamic-update-slice_fusion.3), channel_id=1, source_target_pairs={{0,1},{1,2},{2,3},{4,5},{5,6},{6,7},{8,9},{9,10},{10,11},{12,13},{... | collective-permute-start | bytes 1179656 | tf_op jit(solution)/shard_map/ppermute | solution.py:17
  105.0 3.5 %collective-permute-done.13 = bf16[2,6,128,128]{3,2,1,0:T(8,128)(2,1)S(1)} collective-permute-done((bf16[2,6,128,128]{3,2,1,0:T(8,128)(2,1)S(1)}, bf16[2,6,128,128]{3,2,1,0:T(8,128)(2,1)S(1)}, u32[]{:S(2)}, u32[]{:S(2)}) %collective-permute-start.13) | collective-permute-done | bytes 393248 | tf_op jit(solution)/shard_map/ppermute | solution.py:18
  109.8 1.6 gather_fusion.2
  111.5 1.7 fusion.2
  113.2 8.4 %all_gather.18 = bf16[8,256,128]{2,1,0:T(8,128)(2,1)S(1)} all-gather(bf16[2,256,128]{2,1,0:T(8,128)(2,1)S(1)} %fusion.18), channel_id=1, replica_groups=mesh['horiz'=8,'vert'=4] {'vert'}, dimensions={0}, use_global_device_ids=true | all-gather | bytes 655360 | tf_op jit(solution)/shard_map/all_gather | solution.py:74
  121.6 1.2 convolution_bitcast_fusion.1
  123.0 2.5 %collective-permute-start.14 = (bf16[256,128]{1,0:T(8,128)(2,1)S(1)}, bf16[256,128]{1,0:T(8,128)(2,1)S(1)}, u32[]{:S(2)}, u32[]{:S(2)}) collective-permute-start(bf16[256,128]{1,0:T(8,128)(2,1)S(1)} %bitcast.92), channel_id=1, source_target_pairs={{0,1},{1,2},{2,3},{4,5},{5,6},{6,7},{8,9},{9,10},{10,11},{12,13},{... | collective-permute-start | bytes 196616 | tf_op jit(solution)/shard_map/ppermute | solution.py:26
  125.6 1.2 collective-permute-done.14
  127.2 4.1 %collective-permute-start.15 = (bf16[2,2,128,128]{3,2,1,0:T(8,128)(2,1)S(1)}, bf16[2,2,128,128]{3,2,1,0:T(8,128)(2,1)S(1)}, u32[]{:S(2)}, u32[]{:S(2)}) collective-permute-start(bf16[2,2,128,128]{3,2,1,0:T(8,128)(2,1)S(1)} %copy.51), channel_id=1, source_target_pairs={{0,4},{4,8},{8,12},{12,16},{16,20},{20,24},{24,28},{1,5},{5,9},{9,... | collective-permute-start | bytes 393224 | tf_op jit(solution)/shard_map/ppermute | solution.py:17
  131.3 1.3 collective-permute-start.16
  132.6 2.0 %collective-permute-done.15 = bf16[2,2,128,128]{3,2,1,0:T(8,128)(2,1)S(1)} collective-permute-done((bf16[2,2,128,128]{3,2,1,0:T(8,128)(2,1)S(1)}, bf16[2,2,128,128]{3,2,1,0:T(8,128)(2,1)S(1)}, u32[]{:S(2)}, u32[]{:S(2)}) %collective-permute-start.15) | collective-permute-done | bytes 131104 | tf_op jit(solution)/shard_map/ppermute | solution.py:17
  134.6 3.8 %collective-permute-done.16 = bf16[2,2,128,128]{3,2,1,0:T(8,128)(2,1)S(1)} collective-permute-done((bf16[2,2,128,128]{3,2,1,0:T(8,128)(2,1)S(1)}, bf16[2,2,128,128]{3,2,1,0:T(8,128)(2,1)S(1)}, u32[]{:S(2)}, u32[]{:S(2)}) %collective-permute-start.16) | collective-permute-done | bytes 131104 | tf_op jit(solution)/shard_map/ppermute | solution.py:18
  138.5 2.5 %collective-permute-start.18 = (bf16[2,6,128,128]{3,2,1,0:T(8,128)(2,1)S(1)}, bf16[2,6,128,128]{3,2,1,0:T(8,128)(2,1)S(1)}, u32[]{:S(2)}, u32[]{:S(2)}) collective-permute-start(bf16[2,6,128,128]{3,2,1,0:T(8,128)(2,1)S(1)} %constant_dynamic-update-slice_fusion.6), channel_id=1, source_target_pairs={{1,0},{2,1},{3,2},{5,4},{6,5},{7,6},{9,8},{10,9},{11,10},{13,12},{... | collective-permute-start | bytes 1179656 | tf_op jit(solution)/shard_map/ppermute | solution.py:18
  141.0 3.8 %collective-permute-start.17 = (bf16[2,6,128,128]{3,2,1,0:T(8,128)(2,1)S(1)}, bf16[2,6,128,128]{3,2,1,0:T(8,128)(2,1)S(1)}, u32[]{:S(2)}, u32[]{:S(2)}) collective-permute-start(bf16[2,6,128,128]{3,2,1,0:T(8,128)(2,1)S(1)} %constant_dynamic-update-slice_fusion.6), channel_id=1, source_target_pairs={{0,1},{1,2},{2,3},{4,5},{5,6},{6,7},{8,9},{9,10},{10,11},{12,13},{... | collective-permute-start | bytes 1179656 | tf_op jit(solution)/shard_map/ppermute | solution.py:17
  144.9 3.3 %collective-permute-done.18 = bf16[2,6,128,128]{3,2,1,0:T(8,128)(2,1)S(1)} collective-permute-done((bf16[2,6,128,128]{3,2,1,0:T(8,128)(2,1)S(1)}, bf16[2,6,128,128]{3,2,1,0:T(8,128)(2,1)S(1)}, u32[]{:S(2)}, u32[]{:S(2)}) %collective-permute-start.18) | collective-permute-done | bytes 393248 | tf_op jit(solution)/shard_map/ppermute | solution.py:18
  149.5 1.6 gather_fusion.3
  151.1 1.6 fusion
  152.9 8.4 %all_gather.19 = bf16[8,256,128]{2,1,0:T(8,128)(2,1)S(1)} all-gather(bf16[2,256,128]{2,1,0:T(8,128)(2,1)S(1)} %fusion.19), channel_id=1, replica_groups=mesh['horiz'=8,'vert'=4] {'vert'}, dimensions={0}, use_global_device_ids=true | all-gather | bytes 655360 | tf_op jit(solution)/shard_map/all_gather | solution.py:74
  161.3 1.2 convolution_bitcast_fusion
  162.7 2.5 %collective-permute-start.19 = (bf16[256,128]{1,0:T(8,128)(2,1)S(1)}, bf16[256,128]{1,0:T(8,128)(2,1)S(1)}, u32[]{:S(2)}, u32[]{:S(2)}) collective-permute-start(bf16[256,128]{1,0:T(8,128)(2,1)S(1)} %bitcast.93), channel_id=1, source_target_pairs={{0,1},{1,2},{2,3},{4,5},{5,6},{6,7},{8,9},{9,10},{10,11},{12,13},{... | collective-permute-start | bytes 196616 | tf_op jit(solution)/shard_map/ppermute | solution.py:26
  165.3 1.2 collective-permute-done.19
  (73 shorter events, 16.3 us)
Async XLA Ops:
  0.0 33.0 %copy-start = (bf16[2,2,7,128,128]{4,3,2,1,0:T(8,128)(2,1)S(1)}, bf16[2,2,7,128,128]{4,3,2,1,0:T(8,128)(2,1)}, u32[]{:S(2)}) copy-start(bf16[2,2,7,128,128]{4,3,2,1,0:T(8,128)(2,1)} %param.9) | copy-start | bytes 2752516
  0.0 20.0 %copy-start.1 = (bf16[2,256,128]{2,1,0:T(8,128)(2,1)S(1)}, bf16[2,256,128]{2,1,0:T(8,128)(2,1)}, u32[]{:S(2)}) copy-start(bf16[2,256,128]{2,1,0:T(8,128)(2,1)} %param.8) | copy-start | bytes 393220
  0.0 20.0 %collective-permute-start.1 = (bf16[2,2,128,128]{3,2,1,0:T(8,128)(2,1)}, bf16[2,2,128,128]{3,2,1,0:T(8,128)(2,1)S(1)}, u32[]{:S(2)}, u32[]{:S(2)}) collective-permute-start(bf16[2,2,128,128]{3,2,1,0:T(8,128)(2,1)} %bitcast.82), channel_id=1, source_target_pairs={{4,0},{8,4},{12,8},{16,12},{20,16},{24,20},{28,24},{5,1},{9,5},{13... | collective-permute-start | bytes 393224 | tf_op jit(solution)/shard_map/ppermute | solution.py:18
  1.4 18.6 %collective-permute-start = (bf16[2,2,128,128]{3,2,1,0:T(8,128)(2,1)}, bf16[2,2,128,128]{3,2,1,0:T(8,128)(2,1)S(1)}, u32[]{:S(2)}, u32[]{:S(2)}) collective-permute-start(bf16[2,2,128,128]{3,2,1,0:T(8,128)(2,1)} %bitcast.83), channel_id=1, source_target_pairs={{0,4},{4,8},{8,12},{12,16},{16,20},{20,24},{24,28},{1,5},{5,9},{9,... | collective-permute-start | bytes 393224 | tf_op jit(solution)/shard_map/ppermute | solution.py:17
  7.7 17.9 %copy-start.5 = (s32[2,2]{1,0:T(2,128)S(1)}, s32[2,2]{1,0:T(2,128)}, u32[]{:S(2)}) copy-start(s32[2,2]{1,0:T(2,128)} %param.11) | copy-start | bytes 52
  7.7 18.0 %copy-start.4 = (s32[2,256]{1,0:T(2,128)S(1)}, s32[2,256]{1,0:T(2,128)}, u32[]{:S(2)}) copy-start(s32[2,256]{1,0:T(2,128)} %param.15) | copy-start | bytes 6148
  20.0 9.2 %copy-start.2 = (bf16[2,2,128,128]{3,2,1,0:T(8,128)(2,1)}, bf16[2,2,128,128]{3,2,1,0:T(8,128)(2,1)S(1)}, u32[]{:S(2)}) copy-start(bf16[2,2,128,128]{3,2,1,0:T(8,128)(2,1)S(1)} %collective-permute-done) | copy-start | bytes 393220
  20.1 9.1 %collective-permute-start.3 = (bf16[2,6,128,128]{3,2,1,0:T(8,128)(2,1)S(1)}, bf16[2,6,128,128]{3,2,1,0:T(8,128)(2,1)S(1)}, u32[]{:S(2)}, u32[]{:S(2)}) collective-permute-start(bf16[2,6,128,128]{3,2,1,0:T(8,128)(2,1)S(1)} %pad_maximum_fusion.4), channel_id=1, source_target_pairs={{1,0},{2,1},{3,2},{5,4},{6,5},{7,6},{9,8},{10,9},{11,10},{13,12},{... | collective-permute-start | bytes 1179656 | tf_op jit(solution)/shard_map/ppermute | solution.py:18
  22.1 8.2 %collective-permute-start.2 = (bf16[2,6,128,128]{3,2,1,0:T(8,128)(2,1)S(1)}, bf16[2,6,128,128]{3,2,1,0:T(8,128)(2,1)S(1)}, u32[]{:S(2)}, u32[]{:S(2)}) collective-permute-start(bf16[2,6,128,128]{3,2,1,0:T(8,128)(2,1)S(1)} %pad_maximum_fusion.4), channel_id=1, source_target_pairs={{0,1},{1,2},{2,3},{4,5},{5,6},{6,7},{8,9},{9,10},{10,11},{12,13},{... | collective-permute-start | bytes 1179656 | tf_op jit(solution)/shard_map/ppermute | solution.py:17
  34.8 12.3 %copy-start.3 = (f32[128]{0:T(128)S(1)}, f32[128]{0:T(128)}, u32[]{:S(2)}) copy-start(f32[128]{0:T(128)} %param.14) | copy-start | bytes 1540
  44.6 3.8 %collective-permute-start.4 = (bf16[256,128]{1,0:T(8,128)(2,1)S(1)}, bf16[256,128]{1,0:T(8,128)(2,1)S(1)}, u32[]{:S(2)}, u32[]{:S(2)}) collective-permute-start(bf16[256,128]{1,0:T(8,128)(2,1)S(1)} %bitcast.90), channel_id=1, source_target_pairs={{0,1},{1,2},{2,3},{4,5},{5,6},{6,7},{8,9},{9,10},{10,11},{12,13},{... | collective-permute-start | bytes 196616 | tf_op jit(solution)/shard_map/ppermute | solution.py:26
  48.8 7.3 %collective-permute-start.5 = (bf16[2,2,128,128]{3,2,1,0:T(8,128)(2,1)S(1)}, bf16[2,2,128,128]{3,2,1,0:T(8,128)(2,1)S(1)}, u32[]{:S(2)}, u32[]{:S(2)}) collective-permute-start(bf16[2,2,128,128]{3,2,1,0:T(8,128)(2,1)S(1)} %copy.42), channel_id=1, source_target_pairs={{0,4},{4,8},{8,12},{12,16},{16,20},{20,24},{24,28},{1,5},{5,9},{9,... | collective-permute-start | bytes 393224 | tf_op jit(solution)/shard_map/ppermute | solution.py:17
  52.9 7.2 %collective-permute-start.6 = (bf16[2,2,128,128]{3,2,1,0:T(8,128)(2,1)S(1)}, bf16[2,2,128,128]{3,2,1,0:T(8,128)(2,1)S(1)}, u32[]{:S(2)}, u32[]{:S(2)}) collective-permute-start(bf16[2,2,128,128]{3,2,1,0:T(8,128)(2,1)S(1)} %copy.42), channel_id=1, source_target_pairs={{4,0},{8,4},{12,8},{16,12},{20,16},{24,20},{28,24},{5,1},{9,5},{13... | collective-permute-start | bytes 393224 | tf_op jit(solution)/shard_map/ppermute | solution.py:18
  60.1 9.7 %collective-permute-start.8 = (bf16[2,6,128,128]{3,2,1,0:T(8,128)(2,1)S(1)}, bf16[2,6,128,128]{3,2,1,0:T(8,128)(2,1)S(1)}, u32[]{:S(2)}, u32[]{:S(2)}) collective-permute-start(bf16[2,6,128,128]{3,2,1,0:T(8,128)(2,1)S(1)} %constant_dynamic-update-slice_fusion), channel_id=1, source_target_pairs={{1,0},{2,1},{3,2},{5,4},{6,5},{7,6},{9,8},{10,9},{11,10},{13,12},{... | collective-permute-start | bytes 1179656 | tf_op jit(solution)/shard_map/ppermute | solution.py:18
  62.6 8.3 %collective-permute-start.7 = (bf16[2,6,128,128]{3,2,1,0:T(8,128)(2,1)S(1)}, bf16[2,6,128,128]{3,2,1,0:T(8,128)(2,1)S(1)}, u32[]{:S(2)}, u32[]{:S(2)}) collective-permute-start(bf16[2,6,128,128]{3,2,1,0:T(8,128)(2,1)S(1)} %constant_dynamic-update-slice_fusion), channel_id=1, source_target_pairs={{0,1},{1,2},{2,3},{4,5},{5,6},{6,7},{8,9},{9,10},{10,11},{12,13},{... | collective-permute-start | bytes 1179656 | tf_op jit(solution)/shard_map/ppermute | solution.py:17
  84.2 3.8 %collective-permute-start.9 = (bf16[256,128]{1,0:T(8,128)(2,1)S(1)}, bf16[256,128]{1,0:T(8,128)(2,1)S(1)}, u32[]{:S(2)}, u32[]{:S(2)}) collective-permute-start(bf16[256,128]{1,0:T(8,128)(2,1)S(1)} %bitcast.91), channel_id=1, source_target_pairs={{0,1},{1,2},{2,3},{4,5},{5,6},{6,7},{8,9},{9,10},{10,11},{12,13},{... | collective-permute-start | bytes 196616 | tf_op jit(solution)/shard_map/ppermute | solution.py:26
  88.5 6.4 %collective-permute-start.10 = (bf16[2,2,128,128]{3,2,1,0:T(8,128)(2,1)S(1)}, bf16[2,2,128,128]{3,2,1,0:T(8,128)(2,1)S(1)}, u32[]{:S(2)}, u32[]{:S(2)}) collective-permute-start(bf16[2,2,128,128]{3,2,1,0:T(8,128)(2,1)S(1)} %copy.47), channel_id=1, source_target_pairs={{0,4},{4,8},{8,12},{12,16},{16,20},{20,24},{24,28},{1,5},{5,9},{9,... | collective-permute-start | bytes 393224 | tf_op jit(solution)/shard_map/ppermute | solution.py:17
  91.6 7.2 %collective-permute-start.11 = (bf16[2,2,128,128]{3,2,1,0:T(8,128)(2,1)S(1)}, bf16[2,2,128,128]{3,2,1,0:T(8,128)(2,1)S(1)}, u32[]{:S(2)}, u32[]{:S(2)}) collective-permute-start(bf16[2,2,128,128]{3,2,1,0:T(8,128)(2,1)S(1)} %copy.47), channel_id=1, source_target_pairs={{4,0},{8,4},{12,8},{16,12},{20,16},{24,20},{28,24},{5,1},{9,5},{13... | collective-permute-start | bytes 393224 | tf_op jit(solution)/shard_map/ppermute | solution.py:18
  98.8 9.7 %collective-permute-start.13 = (bf16[2,6,128,128]{3,2,1,0:T(8,128)(2,1)S(1)}, bf16[2,6,128,128]{3,2,1,0:T(8,128)(2,1)S(1)}, u32[]{:S(2)}, u32[]{:S(2)}) collective-permute-start(bf16[2,6,128,128]{3,2,1,0:T(8,128)(2,1)S(1)} %constant_dynamic-update-slice_fusion.3), channel_id=1, source_target_pairs={{1,0},{2,1},{3,2},{5,4},{6,5},{7,6},{9,8},{10,9},{11,10},{13,12},{... | collective-permute-start | bytes 1179656 | tf_op jit(solution)/shard_map/ppermute | solution.py:18
  101.4 8.3 %collective-permute-start.12 = (bf16[2,6,128,128]{3,2,1,0:T(8,128)(2,1)S(1)}, bf16[2,6,128,128]{3,2,1,0:T(8,128)(2,1)S(1)}, u32[]{:S(2)}, u32[]{:S(2)}) collective-permute-start(bf16[2,6,128,128]{3,2,1,0:T(8,128)(2,1)S(1)} %constant_dynamic-update-slice_fusion.3), channel_id=1, source_target_pairs={{0,1},{1,2},{2,3},{4,5},{5,6},{6,7},{8,9},{9,10},{10,11},{12,13},{... | collective-permute-start | bytes 1179656 | tf_op jit(solution)/shard_map/ppermute | solution.py:17
  123.0 3.8 %collective-permute-start.14 = (bf16[256,128]{1,0:T(8,128)(2,1)S(1)}, bf16[256,128]{1,0:T(8,128)(2,1)S(1)}, u32[]{:S(2)}, u32[]{:S(2)}) collective-permute-start(bf16[256,128]{1,0:T(8,128)(2,1)S(1)} %bitcast.92), channel_id=1, source_target_pairs={{0,1},{1,2},{2,3},{4,5},{5,6},{6,7},{8,9},{9,10},{10,11},{12,13},{... | collective-permute-start | bytes 196616 | tf_op jit(solution)/shard_map/ppermute | solution.py:26
  127.2 7.3 %collective-permute-start.15 = (bf16[2,2,128,128]{3,2,1,0:T(8,128)(2,1)S(1)}, bf16[2,2,128,128]{3,2,1,0:T(8,128)(2,1)S(1)}, u32[]{:S(2)}, u32[]{:S(2)}) collective-permute-start(bf16[2,2,128,128]{3,2,1,0:T(8,128)(2,1)S(1)} %copy.51), channel_id=1, source_target_pairs={{0,4},{4,8},{8,12},{12,16},{16,20},{20,24},{24,28},{1,5},{5,9},{9,... | collective-permute-start | bytes 393224 | tf_op jit(solution)/shard_map/ppermute | solution.py:17
  131.3 7.2 %collective-permute-start.16 = (bf16[2,2,128,128]{3,2,1,0:T(8,128)(2,1)S(1)}, bf16[2,2,128,128]{3,2,1,0:T(8,128)(2,1)S(1)}, u32[]{:S(2)}, u32[]{:S(2)}) collective-permute-start(bf16[2,2,128,128]{3,2,1,0:T(8,128)(2,1)S(1)} %copy.51), channel_id=1, source_target_pairs={{4,0},{8,4},{12,8},{16,12},{20,16},{24,20},{28,24},{5,1},{9,5},{13... | collective-permute-start | bytes 393224 | tf_op jit(solution)/shard_map/ppermute | solution.py:18
  138.5 9.7 %collective-permute-start.18 = (bf16[2,6,128,128]{3,2,1,0:T(8,128)(2,1)S(1)}, bf16[2,6,128,128]{3,2,1,0:T(8,128)(2,1)S(1)}, u32[]{:S(2)}, u32[]{:S(2)}) collective-permute-start(bf16[2,6,128,128]{3,2,1,0:T(8,128)(2,1)S(1)} %constant_dynamic-update-slice_fusion.6), channel_id=1, source_target_pairs={{1,0},{2,1},{3,2},{5,4},{6,5},{7,6},{9,8},{10,9},{11,10},{13,12},{... | collective-permute-start | bytes 1179656 | tf_op jit(solution)/shard_map/ppermute | solution.py:18
  141.0 8.3 %collective-permute-start.17 = (bf16[2,6,128,128]{3,2,1,0:T(8,128)(2,1)S(1)}, bf16[2,6,128,128]{3,2,1,0:T(8,128)(2,1)S(1)}, u32[]{:S(2)}, u32[]{:S(2)}) collective-permute-start(bf16[2,6,128,128]{3,2,1,0:T(8,128)(2,1)S(1)} %constant_dynamic-update-slice_fusion.6), channel_id=1, source_target_pairs={{0,1},{1,2},{2,3},{4,5},{5,6},{6,7},{8,9},{9,10},{10,11},{12,13},{... | collective-permute-start | bytes 1179656 | tf_op jit(solution)/shard_map/ppermute | solution.py:17
  162.7 3.8 %collective-permute-start.19 = (bf16[256,128]{1,0:T(8,128)(2,1)S(1)}, bf16[256,128]{1,0:T(8,128)(2,1)S(1)}, u32[]{:S(2)}, u32[]{:S(2)}) collective-permute-start(bf16[256,128]{1,0:T(8,128)(2,1)S(1)} %bitcast.93), channel_id=1, source_target_pairs={{0,1},{1,2},{2,3},{4,5},{5,6},{6,7},{8,9},{9,10},{10,11},{12,13},{... | collective-permute-start | bytes 196616 | tf_op jit(solution)/shard_map/ppermute | solution.py:26
where the time goes:
time: 169 us; the launch traced here: 168 us
  starting transfers between devices  55.3 us (33%)
  blocking collectives  44.9 us (27%)
  waiting for transfers between devices  40.7 us (24%)
  matrix products  11.4 us (7%)
  local copies, waits for them, and re-layouts  9.57 us (6%)
  other arithmetic  5.1 us (3%)
    all_gather x4, blocking collectives, on_device(): lax.all_gather(loaded, 'vert', axis=0, tiled=True).astype(jnp.float32)  33.6 us
    ppermute x8, starting transfers between devices, extended(): before = lax.ppermute(last, axis, up)  30.4 us
    ppermute x8, waiting for transfers between devices, extended(): after = lax.ppermute(leading, axis, down)  25.3 us
    ppermute x8, starting transfers between devices, extended(): after = lax.ppermute(leading, axis, down)  14.9 us
    all_gather x1, blocking collectives, on_device(): all_columns = lax.all_gather(implicit_columns, 'vert', axis=0, tiled=True)  11.3 us
    ppermute x8, waiting for transfers between devices, extended(): before = lax.ppermute(last, axis, up)  10.7 us
    ppermute x4, starting transfers between devices, from_behind(): lax.ppermute(value, axis, [(source, source + steps) for source in range(l...  10 us
    dot_general x4, matrix products, on_device(): jnp.einsum('ltjab,ltjbs->ltas', explicit_tiles, picked, preferred_element...  6.59 us
  transfers between devices with their start and end apart: 20, of which 18 were waited for; matrix products, arithmetic and copies ran while one was open for 2% of the time, Pallas kernels for 0%

commit v1 on v0

--- a/solution.py
+++ b/solution.py
@@ -54,7 +54,16 @@
     source = surface_source.astype(jnp.float32)
     fall_rate = settling[None, None, :]
     wet_cells = wet_mask.astype(jnp.bfloat16)[:, :, None]
-    all_columns = lax.all_gather(implicit_columns, "vert", axis=0, tiled=True)
+    plain = lax.axis_size("vert")
+    reached, a_now, kept_arr = (plain, lax.axis_index("vert"), implicit_columns.shape[0])
+    spare, a_next = (implicit_columns, 1)
+    while a_next < reached:
+        d_next = lax.ppermute(
+            spare, "vert", [(jj, (jj - a_next) % reached) for jj in range(reached)]
+        )
+        spare = jnp.concatenate([spare, d_next], axis=0)
+        a_next = 2 * a_next
+    all_columns = jnp.roll(spare, a_now * kept_arr, axis=0)
     own_rows = lax.dynamic_slice_in_dim(all_columns, first_level, lev_dev, 1)
     current = tracer
     for step_index in range(STEPS):

time: 169 us -> 157 us (0.929)
  blocking collectives: 44.9 us -> 33 us
  local copies, waits for them, and re-layouts: 9.57 us -> 5.37 us
  other arithmetic: 5.1 us -> 8.29 us
  matrix products: 11.4 us -> 8.65 us
  starting transfers between devices: 55.3 us -> 58 us
    all_gather x1 -> x0, blocking collectives: 11.3 us -> none  [on_device(): all_columns = lax.all_gather(implicit_columns, 'vert', axis=0, tiled=True)]
    ppermute x0 -> x2, waiting for transfers between devices: none -> 3.63 us  [on_device(): lax.ppermute(spare, 'vert', [(jj, (jj - a_next) % reached) for jj in rang...]
    gather x4, local copies, waits for them, and re-layouts: 6.5 us -> 2.89 us  [on_device(): picked = flattened[position] * live_slots[:, :, :, None, None]]
    ppermute x8, waiting for transfers between devices: 25.3 us -> 22.1 us  [extended(): after = lax.ppermute(leading, axis, down)]
    dot_general x4, matrix products: 6.59 us -> 3.92 us  [on_device(): jnp.einsum('ltjab,ltjbs->ltas', explicit_tiles, picked, preferred_element...]
  transfers between devices with their start and end apart: 20 -> 22, of which waited for: 18 -> 18; matrix products, arithmetic and copies ran while one was open for 2% -> 4% of each run, Pallas kernels for 0% -> 0%
where the time goes in v1:
time: 157 us; the launch traced here: 155 us
  starting transfers between devices  58 us (37%)
  waiting for transfers between devices  41 us (26%)
  blocking collectives  33 us (21%)
  matrix products  8.65 us (6%)
  other arithmetic  8.29 us (5%)
  local copies, waits for them, and re-layouts  5.37 us (3%)
    all_gather x4, blocking collectives, on_device(): lax.all_gather(loaded, 'vert', axis=0, tiled=True).astype(jnp.float32)  33 us
    ppermute x8, starting transfers between devices, extended(): before = lax.ppermute(last, axis, up)  31.3 us
    ppermute x8, waiting for transfers between devices, extended(): after = lax.ppermute(leading, axis, down)  22.1 us
    ppermute x8, starting transfers between devices, extended(): after = lax.ppermute(leading, axis, down)  14.7 us
    ppermute x4, starting transfers between devices, from_behind(): lax.ppermute(value, axis, [(source, source + steps) for source in range(l...  10.9 us
    ppermute x8, waiting for transfers between devices, extended(): before = lax.ppermute(last, axis, up)  10.6 us
    dot_general x4, matrix products, on_device(): jnp.einsum('ckm,mcs->kcs', own_rows, lax.all_gather(loaded, 'vert', axis=...  4.73 us
    ppermute x4, waiting for transfers between devices, from_behind(): lax.ppermute(value, axis, [(source, source + steps) for source in range(l...  4.68 us
  transfers between devices with their start and end apart: 22, of which 18 were waited for; matrix products, arithmetic and copies ran while one was open for 4% of the time, Pallas kernels for 0%

profile of v1, /device:TPU:1, one launch (start us, length us, event | category | flops | bytes accessed | tf_op | source)
XLA Modules:
  0.0 154.9 jit_solution(3982645391818163522)
XLA Ops:
  0.0 1.4 collective-permute-start.1
  1.4 4.6 %collective-permute-start = (bf16[2,2,128,128]{3,2,1,0:T(8,128)(2,1)}, bf16[2,2,128,128]{3,2,1,0:T(8,128)(2,1)S(1)}, u32[]{:S(2)}, u32[]{:S(2)}) collective-permute-start(bf16[2,2,128,128]{3,2,1,0:T(8,128)(2,1)} %bitcast.87), channel_id=1, source_target_pairs={{0,4},{4,8},{8,12},{12,16},{16,20},{20,24},{24,28},{1,5},{5,9},{9,... | collective-permute-start | bytes 393224 | tf_op jit(solution)/shard_map/ppermute | solution.py:17
  9.3 2.1 %collective-permute-done = bf16[2,2,128,128]{3,2,1,0:T(8,128)(2,1)S(1)} collective-permute-done((bf16[2,2,128,128]{3,2,1,0:T(8,128)(2,1)}, bf16[2,2,128,128]{3,2,1,0:T(8,128)(2,1)S(1)}, u32[]{:S(2)}, u32[]{:S(2)}) %collective-permute-start) | collective-permute-done | bytes 131104 | tf_op jit(solution)/shard_map/ppermute | solution.py:17
  12.3 2.4 %collective-permute-start.3 = (bf16[2,6,128,128]{3,2,1,0:T(8,128)(2,1)S(1)}, bf16[2,6,128,128]{3,2,1,0:T(8,128)(2,1)S(1)}, u32[]{:S(2)}, u32[]{:S(2)}) collective-permute-start(bf16[2,6,128,128]{3,2,1,0:T(8,128)(2,1)S(1)} %pad_maximum_fusion.4), channel_id=1, source_target_pairs={{1,0},{2,1},{3,2},{5,4},{6,5},{7,6},{9,8},{10,9},{11,10},{13,12},{... | collective-permute-start | bytes 1179656 | tf_op jit(solution)/shard_map/ppermute | solution.py:18
  14.7 3.2 %collective-permute-start.2 = (bf16[2,6,128,128]{3,2,1,0:T(8,128)(2,1)S(1)}, bf16[2,6,128,128]{3,2,1,0:T(8,128)(2,1)}, u32[]{:S(2)}, u32[]{:S(2)}) collective-permute-start(bf16[2,6,128,128]{3,2,1,0:T(8,128)(2,1)S(1)} %pad_maximum_fusion.4), channel_id=1, source_target_pairs={{0,1},{1,2},{2,3},{4,5},{5,6},{6,7},{8,9},{9,10},{10,11},{12,13},{... | collective-permute-start | bytes 1179656 | tf_op jit(solution)/shard_map/ppermute | solution.py:17
  19.7 3.6 %collective-permute-done.5 = f32[128,8,8]{0,2,1:T(8,128)S(1)} collective-permute-done((f32[128,8,8]{0,2,1:T(8,128)S(1)}, f32[128,8,8]{0,2,1:T(8,128)S(1)}, u32[]{:S(2)}, u32[]{:S(2)}) %collective-permute-start.5) | collective-permute-done | bytes 32800 | tf_op jit(solution)/shard_map/ppermute | solution.py:61
  23.7 1.1 pad_maximum_fusion
  26.1 7.8 %all_gather.12 = bf16[8,256,128]{2,1,0:T(8,128)(2,1)S(1)} all-gather(bf16[2,256,128]{2,1,0:T(8,128)(2,1)S(1)} %fusion.16), channel_id=1, replica_groups=mesh['horiz'=8,'vert'=4] {'vert'}, dimensions={0}, use_global_device_ids=true | all-gather | bytes 655360 | tf_op jit(solution)/shard_map/all_gather | solution.py:83
  33.9 1.2 convolution_bitcast_fusion.3
  35.3 3.4 %collective-permute-start.6 = (bf16[256,128]{1,0:T(8,128)(2,1)S(1)}, bf16[256,128]{1,0:T(8,128)(2,1)S(1)}, u32[]{:S(2)}, u32[]{:S(2)}) collective-permute-start(bf16[256,128]{1,0:T(8,128)(2,1)S(1)} %bitcast.94), channel_id=1, source_target_pairs={{0,1},{1,2},{2,3},{4,5},{5,6},{6,7},{8,9},{9,10},{10,11},{12,13},{... | collective-permute-start | bytes 196616 | tf_op jit(solution)/shard_map/ppermute | solution.py:26
  40.4 4.0 %collective-permute-start.7 = (bf16[2,2,128,128]{3,2,1,0:T(8,128)(2,1)S(1)}, bf16[2,2,128,128]{3,2,1,0:T(8,128)(2,1)S(1)}, u32[]{:S(2)}, u32[]{:S(2)}) collective-permute-start(bf16[2,2,128,128]{3,2,1,0:T(8,128)(2,1)S(1)} %copy.48), channel_id=1, source_target_pairs={{0,4},{4,8},{8,12},{12,16},{16,20},{20,24},{24,28},{1,5},{5,9},{9,... | collective-permute-start | bytes 393224 | tf_op jit(solution)/shard_map/ppermute | solution.py:17
  44.5 1.3 collective-permute-start.8
  46.8 4.0 %collective-permute-done.8 = bf16[2,2,128,128]{3,2,1,0:T(8,128)(2,1)S(1)} collective-permute-done((bf16[2,2,128,128]{3,2,1,0:T(8,128)(2,1)S(1)}, bf16[2,2,128,128]{3,2,1,0:T(8,128)(2,1)S(1)}, u32[]{:S(2)}, u32[]{:S(2)}) %collective-permute-start.8) | collective-permute-done | bytes 131104 | tf_op jit(solution)/shard_map/ppermute | solution.py:18
  50.9 2.0 %collective-permute-start.10 = (bf16[2,6,128,128]{3,2,1,0:T(8,128)(2,1)S(1)}, bf16[2,6,128,128]{3,2,1,0:T(8,128)(2,1)S(1)}, u32[]{:S(2)}, u32[]{:S(2)}) collective-permute-start(bf16[2,6,128,128]{3,2,1,0:T(8,128)(2,1)S(1)} %constant_dynamic-update-slice_fusion), channel_id=1, source_target_pairs={{1,0},{2,1},{3,2},{5,4},{6,5},{7,6},{9,8},{10,9},{11,10},{13,12},{... | collective-permute-start | bytes 1179656 | tf_op jit(solution)/shard_map/ppermute | solution.py:18
  52.9 5.0 %collective-permute-start.9 = (bf16[2,6,128,128]{3,2,1,0:T(8,128)(2,1)S(1)}, bf16[2,6,128,128]{3,2,1,0:T(8,128)(2,1)S(1)}, u32[]{:S(2)}, u32[]{:S(2)}) collective-permute-start(bf16[2,6,128,128]{3,2,1,0:T(8,128)(2,1)S(1)} %constant_dynamic-update-slice_fusion), channel_id=1, source_target_pairs={{0,1},{1,2},{2,3},{4,5},{5,6},{6,7},{8,9},{9,10},{10,11},{12,13},{... | collective-permute-start | bytes 1179656 | tf_op jit(solution)/shard_map/ppermute | solution.py:17
  57.8 3.5 %collective-permute-done.10 = bf16[2,6,128,128]{3,2,1,0:T(8,128)(2,1)S(1)} collective-permute-done((bf16[2,6,128,128]{3,2,1,0:T(8,128)(2,1)S(1)}, bf16[2,6,128,128]{3,2,1,0:T(8,128)(2,1)S(1)}, u32[]{:S(2)}, u32[]{:S(2)}) %collective-permute-start.10) | collective-permute-done | bytes 393248 | tf_op jit(solution)/shard_map/ppermute | solution.py:18
  61.3 1.2 collective-permute-done.9
  63.4 1.2 fusion.4
  64.7 8.4 %all_gather.13 = bf16[8,256,128]{2,1,0:T(8,128)(2,1)S(1)} all-gather(bf16[2,256,128]{2,1,0:T(8,128)(2,1)S(1)} %fusion.17), channel_id=1, replica_groups=mesh['horiz'=8,'vert'=4] {'vert'}, dimensions={0}, use_global_device_ids=true | all-gather | bytes 655360 | tf_op jit(solution)/shard_map/all_gather | solution.py:83
  73.0 1.2 convolution_bitcast_fusion.2
  74.4 2.5 %collective-permute-start.11 = (bf16[256,128]{1,0:T(8,128)(2,1)S(1)}, bf16[256,128]{1,0:T(8,128)(2,1)S(1)}, u32[]{:S(2)}, u32[]{:S(2)}) collective-permute-start(bf16[256,128]{1,0:T(8,128)(2,1)S(1)} %bitcast.95), channel_id=1, source_target_pairs={{0,1},{1,2},{2,3},{4,5},{5,6},{6,7},{8,9},{9,10},{10,11},{12,13},{... | collective-permute-start | bytes 196616 | tf_op jit(solution)/shard_map/ppermute | solution.py:26
  77.0 1.2 collective-permute-done.11
  78.7 4.1 %collective-permute-start.12 = (bf16[2,2,128,128]{3,2,1,0:T(8,128)(2,1)S(1)}, bf16[2,2,128,128]{3,2,1,0:T(8,128)(2,1)S(1)}, u32[]{:S(2)}, u32[]{:S(2)}) collective-permute-start(bf16[2,2,128,128]{3,2,1,0:T(8,128)(2,1)S(1)} %copy.53), channel_id=1, source_target_pairs={{0,4},{4,8},{8,12},{12,16},{16,20},{20,24},{24,28},{1,5},{5,9},{9,... | collective-permute-start | bytes 393224 | tf_op jit(solution)/shard_map/ppermute | solution.py:17
  82.8 1.3 collective-permute-start.13
  84.1 2.0 %collective-permute-done.12 = bf16[2,2,128,128]{3,2,1,0:T(8,128)(2,1)S(1)} collective-permute-done((bf16[2,2,128,128]{3,2,1,0:T(8,128)(2,1)S(1)}, bf16[2,2,128,128]{3,2,1,0:T(8,128)(2,1)S(1)}, u32[]{:S(2)}, u32[]{:S(2)}) %collective-permute-start.12) | collective-permute-done | bytes 131104 | tf_op jit(solution)/shard_map/ppermute | solution.py:17
  86.2 3.8 %collective-permute-done.13 = bf16[2,2,128,128]{3,2,1,0:T(8,128)(2,1)S(1)} collective-permute-done((bf16[2,2,128,128]{3,2,1,0:T(8,128)(2,1)S(1)}, bf16[2,2,128,128]{3,2,1,0:T(8,128)(2,1)S(1)}, u32[]{:S(2)}, u32[]{:S(2)}) %collective-permute-start.13) | collective-permute-done | bytes 131104 | tf_op jit(solution)/shard_map/ppermute | solution.py:18
  90.0 2.5 %collective-permute-start.15 = (bf16[2,6,128,128]{3,2,1,0:T(8,128)(2,1)S(1)}, bf16[2,6,128,128]{3,2,1,0:T(8,128)(2,1)S(1)}, u32[]{:S(2)}, u32[]{:S(2)}) collective-permute-start(bf16[2,6,128,128]{3,2,1,0:T(8,128)(2,1)S(1)} %constant_dynamic-update-slice_fusion.3), channel_id=1, source_target_pairs={{1,0},{2,1},{3,2},{5,4},{6,5},{7,6},{9,8},{10,9},{11,10},{13,12},{... | collective-permute-start | bytes 1179656 | tf_op jit(solution)/shard_map/ppermute | solution.py:18
  92.6 3.6 %collective-permute-start.14 = (bf16[2,6,128,128]{3,2,1,0:T(8,128)(2,1)S(1)}, bf16[2,6,128,128]{3,2,1,0:T(8,128)(2,1)S(1)}, u32[]{:S(2)}, u32[]{:S(2)}) collective-permute-start(bf16[2,6,128,128]{3,2,1,0:T(8,128)(2,1)S(1)} %constant_dynamic-update-slice_fusion.3), channel_id=1, source_target_pairs={{0,1},{1,2},{2,3},{4,5},{5,6},{6,7},{8,9},{9,10},{10,11},{12,13},{... | collective-permute-start | bytes 1179656 | tf_op jit(solution)/shard_map/ppermute | solution.py:17
  96.2 3.5 %collective-permute-done.15 = bf16[2,6,128,128]{3,2,1,0:T(8,128)(2,1)S(1)} collective-permute-done((bf16[2,6,128,128]{3,2,1,0:T(8,128)(2,1)S(1)}, bf16[2,6,128,128]{3,2,1,0:T(8,128)(2,1)S(1)}, u32[]{:S(2)}, u32[]{:S(2)}) %collective-permute-start.15) | collective-permute-done | bytes 393248 | tf_op jit(solution)/shard_map/ppermute | solution.py:18
  99.7 1.2 collective-permute-done.14
  101.7 1.1 fusion.2
  103.0 8.4 %all_gather.14 = bf16[8,256,128]{2,1,0:T(8,128)(2,1)S(1)} all-gather(bf16[2,256,128]{2,1,0:T(8,128)(2,1)S(1)} %fusion.18), channel_id=1, replica_groups=mesh['horiz'=8,'vert'=4] {'vert'}, dimensions={0}, use_global_device_ids=true | all-gather | bytes 655360 | tf_op jit(solution)/shard_map/all_gather | solution.py:83
  111.4 1.2 convolution_bitcast_fusion.1
  112.8 2.5 %collective-permute-start.16 = (bf16[256,128]{1,0:T(8,128)(2,1)S(1)}, bf16[256,128]{1,0:T(8,128)(2,1)S(1)}, u32[]{:S(2)}, u32[]{:S(2)}) collective-permute-start(bf16[256,128]{1,0:T(8,128)(2,1)S(1)} %bitcast.96), channel_id=1, source_target_pairs={{0,1},{1,2},{2,3},{4,5},{5,6},{6,7},{8,9},{9,10},{10,11},{12,13},{... | collective-permute-start | bytes 196616 | tf_op jit(solution)/shard_map/ppermute | solution.py:26
  115.4 1.2 collective-permute-done.16
  117.0 3.0 %collective-permute-start.17 = (bf16[2,2,128,128]{3,2,1,0:T(8,128)(2,1)S(1)}, bf16[2,2,128,128]{3,2,1,0:T(8,128)(2,1)S(1)}, u32[]{:S(2)}, u32[]{:S(2)}) collective-permute-start(bf16[2,2,128,128]{3,2,1,0:T(8,128)(2,1)S(1)} %copy.57), channel_id=1, source_target_pairs={{0,4},{4,8},{8,12},{12,16},{16,20},{20,24},{24,28},{1,5},{5,9},{9,... | collective-permute-start | bytes 393224 | tf_op jit(solution)/shard_map/ppermute | solution.py:17
  120.1 1.3 collective-permute-start.18
  121.4 2.0 %collective-permute-done.17 = bf16[2,2,128,128]{3,2,1,0:T(8,128)(2,1)S(1)} collective-permute-done((bf16[2,2,128,128]{3,2,1,0:T(8,128)(2,1)S(1)}, bf16[2,2,128,128]{3,2,1,0:T(8,128)(2,1)S(1)}, u32[]{:S(2)}, u32[]{:S(2)}) %collective-permute-start.17) | collective-permute-done | bytes 131104 | tf_op jit(solution)/shard_map/ppermute | solution.py:17
  123.4 3.8 %collective-permute-done.18 = bf16[2,2,128,128]{3,2,1,0:T(8,128)(2,1)S(1)} collective-permute-done((bf16[2,2,128,128]{3,2,1,0:T(8,128)(2,1)S(1)}, bf16[2,2,128,128]{3,2,1,0:T(8,128)(2,1)S(1)}, u32[]{:S(2)}, u32[]{:S(2)}) %collective-permute-start.18) | collective-permute-done | bytes 131104 | tf_op jit(solution)/shard_map/ppermute | solution.py:18
  127.3 2.5 %collective-permute-start.20 = (bf16[2,6,128,128]{3,2,1,0:T(8,128)(2,1)S(1)}, bf16[2,6,128,128]{3,2,1,0:T(8,128)(2,1)S(1)}, u32[]{:S(2)}, u32[]{:S(2)}) collective-permute-start(bf16[2,6,128,128]{3,2,1,0:T(8,128)(2,1)S(1)} %constant_dynamic-update-slice_fusion.6), channel_id=1, source_target_pairs={{1,0},{2,1},{3,2},{5,4},{6,5},{7,6},{9,8},{10,9},{11,10},{13,12},{... | collective-permute-start | bytes 1179656 | tf_op jit(solution)/shard_map/ppermute | solution.py:18
  129.8 3.8 %collective-permute-start.19 = (bf16[2,6,128,128]{3,2,1,0:T(8,128)(2,1)S(1)}, bf16[2,6,128,128]{3,2,1,0:T(8,128)(2,1)S(1)}, u32[]{:S(2)}, u32[]{:S(2)}) collective-permute-start(bf16[2,6,128,128]{3,2,1,0:T(8,128)(2,1)S(1)} %constant_dynamic-update-slice_fusion.6), channel_id=1, source_target_pairs={{0,1},{1,2},{2,3},{4,5},{5,6},{6,7},{8,9},{9,10},{10,11},{12,13},{... | collective-permute-start | bytes 1179656 | tf_op jit(solution)/shard_map/ppermute | solution.py:17
  133.6 3.3 %collective-permute-done.20 = bf16[2,6,128,128]{3,2,1,0:T(8,128)(2,1)S(1)} collective-permute-done((bf16[2,6,128,128]{3,2,1,0:T(8,128)(2,1)S(1)}, bf16[2,6,128,128]{3,2,1,0:T(8,128)(2,1)S(1)}, u32[]{:S(2)}, u32[]{:S(2)}) %collective-permute-start.20) | collective-permute-done | bytes 393248 | tf_op jit(solution)/shard_map/ppermute | solution.py:18
  137.0 1.2 collective-permute-done.19
  139.0 1.2 fusion
  140.3 8.4 %all_gather.15 = bf16[8,256,128]{2,1,0:T(8,128)(2,1)S(1)} all-gather(bf16[2,256,128]{2,1,0:T(8,128)(2,1)S(1)} %fusion.19), channel_id=1, replica_groups=mesh['horiz'=8,'vert'=4] {'vert'}, dimensions={0}, use_global_device_ids=true | all-gather | bytes 655360 | tf_op jit(solution)/shard_map/all_gather | solution.py:83
  148.7 1.2 convolution_bitcast_fusion
  150.0 2.5 %collective-permute-start.21 = (bf16[256,128]{1,0:T(8,128)(2,1)S(1)}, bf16[256,128]{1,0:T(8,128)(2,1)S(1)}, u32[]{:S(2)}, u32[]{:S(2)}) collective-permute-start(bf16[256,128]{1,0:T(8,128)(2,1)S(1)} %bitcast.97), channel_id=1, source_target_pairs={{0,1},{1,2},{2,3},{4,5},{5,6},{6,7},{8,9},{9,10},{10,11},{12,13},{... | collective-permute-start | bytes 196616 | tf_op jit(solution)/shard_map/ppermute | solution.py:26
  152.6 1.2 collective-permute-done.21
  (77 shorter events, 16.1 us)
Async XLA Ops:
  0.0 25.5 %copy-start = (bf16[2,2,7,128,128]{4,3,2,1,0:T(8,128)(2,1)S(1)}, bf16[2,2,7,128,128]{4,3,2,1,0:T(8,128)(2,1)}, u32[]{:S(2)}) copy-start(bf16[2,2,7,128,128]{4,3,2,1,0:T(8,128)(2,1)} %param.9) | copy-start | bytes 2752516
  0.0 23.6 %copy-start.1 = (bf16[2,256,128]{2,1,0:T(8,128)(2,1)S(1)}, bf16[2,256,128]{2,1,0:T(8,128)(2,1)}, u32[]{:S(2)}) copy-start(bf16[2,256,128]{2,1,0:T(8,128)(2,1)} %param.8) | copy-start | bytes 393220
  0.0 23.3 %copy-start.2 = (f32[64,8,8]{0,2,1:T(8,128)S(1)}, f32[64,8,8]{0,2,1:T(8,128)}, u32[]{:S(2)}) copy-start(f32[64,8,8]{0,2,1:T(8,128)} %param.13) | copy-start | bytes 49156
  0.0 9.3 %collective-permute-start.1 = (bf16[2,2,128,128]{3,2,1,0:T(8,128)(2,1)}, bf16[2,2,128,128]{3,2,1,0:T(8,128)(2,1)S(1)}, u32[]{:S(2)}, u32[]{:S(2)}) collective-permute-start(bf16[2,2,128,128]{3,2,1,0:T(8,128)(2,1)} %bitcast.86), channel_id=1, source_target_pairs={{4,0},{8,4},{12,8},{16,12},{20,16},{24,20},{28,24},{5,1},{9,5},{13... | collective-permute-start | bytes 393224 | tf_op jit(solution)/shard_map/ppermute | solution.py:18
  1.4 9.9 %collective-permute-start = (bf16[2,2,128,128]{3,2,1,0:T(8,128)(2,1)}, bf16[2,2,128,128]{3,2,1,0:T(8,128)(2,1)S(1)}, u32[]{:S(2)}, u32[]{:S(2)}) collective-permute-start(bf16[2,2,128,128]{3,2,1,0:T(8,128)(2,1)} %bitcast.87), channel_id=1, source_target_pairs={{0,4},{4,8},{8,12},{12,16},{16,20},{20,24},{24,28},{1,5},{5,9},{9,... | collective-permute-start | bytes 393224 | tf_op jit(solution)/shard_map/ppermute | solution.py:17
  6.1 11.8 %collective-permute-start.4 = (f32[64,8,8]{0,2,1:T(8,128)}, f32[64,8,8]{0,2,1:T(8,128)S(1)}, u32[]{:S(2)}, u32[]{:S(2)}) collective-permute-start(f32[64,8,8]{0,2,1:T(8,128)} %param.13), channel_id=1, source_target_pairs={{0,3},{1,0},{2,1},{3,2},{4,7},{5,4},{6,5},{7,6},{8,11},{9,8},{10,9... | collective-permute-start | bytes 49160 | tf_op jit(solution)/shard_map/ppermute | solution.py:61
  9.3 16.7 %copy-start.4 = (bf16[2,2,7]{2,1,0:T(2,128)(2,1)}, bf16[2,2,7]{2,1,0:T(2,128)(2,1)S(1)}, u32[]{:S(2)}) copy-start(bf16[2,2,7]{2,1,0:T(2,128)(2,1)S(1)} %compare_convert_fusion) | copy-start | bytes 172
  12.3 11.3 %collective-permute-start.3 = (bf16[2,6,128,128]{3,2,1,0:T(8,128)(2,1)S(1)}, bf16[2,6,128,128]{3,2,1,0:T(8,128)(2,1)S(1)}, u32[]{:S(2)}, u32[]{:S(2)}) collective-permute-start(bf16[2,6,128,128]{3,2,1,0:T(8,128)(2,1)S(1)} %pad_maximum_fusion.4), channel_id=1, source_target_pairs={{1,0},{2,1},{3,2},{5,4},{6,5},{7,6},{9,8},{10,9},{11,10},{13,12},{... | collective-permute-start | bytes 1179656 | tf_op jit(solution)/shard_map/ppermute | solution.py:18
  14.7 8.9 %collective-permute-start.2 = (bf16[2,6,128,128]{3,2,1,0:T(8,128)(2,1)S(1)}, bf16[2,6,128,128]{3,2,1,0:T(8,128)(2,1)}, u32[]{:S(2)}, u32[]{:S(2)}) collective-permute-start(bf16[2,6,128,128]{3,2,1,0:T(8,128)(2,1)S(1)} %pad_maximum_fusion.4), channel_id=1, source_target_pairs={{0,1},{1,2},{2,3},{4,5},{5,6},{6,7},{8,9},{9,10},{10,11},{12,13},{... | collective-permute-start | bytes 1179656 | tf_op jit(solution)/shard_map/ppermute | solution.py:17
  18.7 4.5 %collective-permute-start.5 = (f32[128,8,8]{0,2,1:T(8,128)S(1)}, f32[128,8,8]{0,2,1:T(8,128)S(1)}, u32[]{:S(2)}, u32[]{:S(2)}) collective-permute-start(f32[128,8,8]{0,2,1:T(8,128)S(1)} %pad_maximum_fusion.5), channel_id=1, source_target_pairs={{0,2},{1,3},{2,0},{3,1},{4,6},{5,7},{6,4},{7,5},{8,10},{9,11},{10,... | collective-permute-start | bytes 98312 | tf_op jit(solution)/shard_map/ppermute | solution.py:61
  26.1 12.6 %copy-start.3 = (f32[128]{0:T(128)S(1)}, f32[128]{0:T(128)}, u32[]{:S(2)}) copy-start(f32[128]{0:T(128)} %param.14) | copy-start | bytes 1540
  35.3 4.7 %collective-permute-start.6 = (bf16[256,128]{1,0:T(8,128)(2,1)S(1)}, bf16[256,128]{1,0:T(8,128)(2,1)S(1)}, u32[]{:S(2)}, u32[]{:S(2)}) collective-permute-start(bf16[256,128]{1,0:T(8,128)(2,1)S(1)} %bitcast.94), channel_id=1, source_target_pairs={{0,1},{1,2},{2,3},{4,5},{5,6},{6,7},{8,9},{9,10},{10,11},{12,13},{... | collective-permute-start | bytes 196616 | tf_op jit(solution)/shard_map/ppermute | solution.py:26
  40.4 6.3 %collective-permute-start.7 = (bf16[2,2,128,128]{3,2,1,0:T(8,128)(2,1)S(1)}, bf16[2,2,128,128]{3,2,1,0:T(8,128)(2,1)S(1)}, u32[]{:S(2)}, u32[]{:S(2)}) collective-permute-start(bf16[2,2,128,128]{3,2,1,0:T(8,128)(2,1)S(1)} %copy.48), channel_id=1, source_target_pairs={{0,4},{4,8},{8,12},{12,16},{16,20},{20,24},{24,28},{1,5},{5,9},{9,... | collective-permute-start | bytes 393224 | tf_op jit(solution)/shard_map/ppermute | solution.py:17
  44.5 6.4 %collective-permute-start.8 = (bf16[2,2,128,128]{3,2,1,0:T(8,128)(2,1)S(1)}, bf16[2,2,128,128]{3,2,1,0:T(8,128)(2,1)S(1)}, u32[]{:S(2)}, u32[]{:S(2)}) collective-permute-start(bf16[2,2,128,128]{3,2,1,0:T(8,128)(2,1)S(1)} %copy.48), channel_id=1, source_target_pairs={{4,0},{8,4},{12,8},{16,12},{20,16},{24,20},{28,24},{5,1},{9,5},{13... | collective-permute-start | bytes 393224 | tf_op jit(solution)/shard_map/ppermute | solution.py:18
  50.9 10.4 %collective-permute-start.10 = (bf16[2,6,128,128]{3,2,1,0:T(8,128)(2,1)S(1)}, bf16[2,6,128,128]{3,2,1,0:T(8,128)(2,1)S(1)}, u32[]{:S(2)}, u32[]{:S(2)}) collective-permute-start(bf16[2,6,128,128]{3,2,1,0:T(8,128)(2,1)S(1)} %constant_dynamic-update-slice_fusion), channel_id=1, source_target_pairs={{1,0},{2,1},{3,2},{5,4},{6,5},{7,6},{9,8},{10,9},{11,10},{13,12},{... | collective-permute-start | bytes 1179656 | tf_op jit(solution)/shard_map/ppermute | solution.py:18
  52.9 9.7 %collective-permute-start.9 = (bf16[2,6,128,128]{3,2,1,0:T(8,128)(2,1)S(1)}, bf16[2,6,128,128]{3,2,1,0:T(8,128)(2,1)S(1)}, u32[]{:S(2)}, u32[]{:S(2)}) collective-permute-start(bf16[2,6,128,128]{3,2,1,0:T(8,128)(2,1)S(1)} %constant_dynamic-update-slice_fusion), channel_id=1, source_target_pairs={{0,1},{1,2},{2,3},{4,5},{5,6},{6,7},{8,9},{9,10},{10,11},{12,13},{... | collective-permute-start | bytes 1179656 | tf_op jit(solution)/shard_map/ppermute | solution.py:17
  74.4 3.8 %collective-permute-start.11 = (bf16[256,128]{1,0:T(8,128)(2,1)S(1)}, bf16[256,128]{1,0:T(8,128)(2,1)S(1)}, u32[]{:S(2)}, u32[]{:S(2)}) collective-permute-start(bf16[256,128]{1,0:T(8,128)(2,1)S(1)} %bitcast.95), channel_id=1, source_target_pairs={{0,1},{1,2},{2,3},{4,5},{5,6},{6,7},{8,9},{9,10},{10,11},{12,13},{... | collective-permute-start | bytes 196616 | tf_op jit(solution)/shard_map/ppermute | solution.py:26
  78.7 7.4 %collective-permute-start.12 = (bf16[2,2,128,128]{3,2,1,0:T(8,128)(2,1)S(1)}, bf16[2,2,128,128]{3,2,1,0:T(8,128)(2,1)S(1)}, u32[]{:S(2)}, u32[]{:S(2)}) collective-permute-start(bf16[2,2,128,128]{3,2,1,0:T(8,128)(2,1)S(1)} %copy.53), channel_id=1, source_target_pairs={{0,4},{4,8},{8,12},{12,16},{16,20},{20,24},{24,28},{1,5},{5,9},{9,... | collective-permute-start | bytes 393224 | tf_op jit(solution)/shard_map/ppermute | solution.py:17
  82.8 7.2 %collective-permute-start.13 = (bf16[2,2,128,128]{3,2,1,0:T(8,128)(2,1)S(1)}, bf16[2,2,128,128]{3,2,1,0:T(8,128)(2,1)S(1)}, u32[]{:S(2)}, u32[]{:S(2)}) collective-permute-start(bf16[2,2,128,128]{3,2,1,0:T(8,128)(2,1)S(1)} %copy.53), channel_id=1, source_target_pairs={{4,0},{8,4},{12,8},{16,12},{20,16},{24,20},{28,24},{5,1},{9,5},{13... | collective-permute-start | bytes 393224 | tf_op jit(solution)/shard_map/ppermute | solution.py:18
  90.0 9.7 %collective-permute-start.15 = (bf16[2,6,128,128]{3,2,1,0:T(8,128)(2,1)S(1)}, bf16[2,6,128,128]{3,2,1,0:T(8,128)(2,1)S(1)}, u32[]{:S(2)}, u32[]{:S(2)}) collective-permute-start(bf16[2,6,128,128]{3,2,1,0:T(8,128)(2,1)S(1)} %constant_dynamic-update-slice_fusion.3), channel_id=1, source_target_pairs={{1,0},{2,1},{3,2},{5,4},{6,5},{7,6},{9,8},{10,9},{11,10},{13,12},{... | collective-permute-start | bytes 1179656 | tf_op jit(solution)/shard_map/ppermute | solution.py:18
  92.6 8.3 %collective-permute-start.14 = (bf16[2,6,128,128]{3,2,1,0:T(8,128)(2,1)S(1)}, bf16[2,6,128,128]{3,2,1,0:T(8,128)(2,1)S(1)}, u32[]{:S(2)}, u32[]{:S(2)}) collective-permute-start(bf16[2,6,128,128]{3,2,1,0:T(8,128)(2,1)S(1)} %constant_dynamic-update-slice_fusion.3), channel_id=1, source_target_pairs={{0,1},{1,2},{2,3},{4,5},{5,6},{6,7},{8,9},{9,10},{10,11},{12,13},{... | collective-permute-start | bytes 1179656 | tf_op jit(solution)/shard_map/ppermute | solution.py:17
  112.8 3.8 %collective-permute-start.16 = (bf16[256,128]{1,0:T(8,128)(2,1)S(1)}, bf16[256,128]{1,0:T(8,128)(2,1)S(1)}, u32[]{:S(2)}, u32[]{:S(2)}) collective-permute-start(bf16[256,128]{1,0:T(8,128)(2,1)S(1)} %bitcast.96), channel_id=1, source_target_pairs={{0,1},{1,2},{2,3},{4,5},{5,6},{6,7},{8,9},{9,10},{10,11},{12,13},{... | collective-permute-start | bytes 196616 | tf_op jit(solution)/shard_map/ppermute | solution.py:26
  117.0 6.3 %collective-permute-start.17 = (bf16[2,2,128,128]{3,2,1,0:T(8,128)(2,1)S(1)}, bf16[2,2,128,128]{3,2,1,0:T(8,128)(2,1)S(1)}, u32[]{:S(2)}, u32[]{:S(2)}) collective-permute-start(bf16[2,2,128,128]{3,2,1,0:T(8,128)(2,1)S(1)} %copy.57), channel_id=1, source_target_pairs={{0,4},{4,8},{8,12},{12,16},{16,20},{20,24},{24,28},{1,5},{5,9},{9,... | collective-permute-start | bytes 393224 | tf_op jit(solution)/shard_map/ppermute | solution.py:17
  120.1 7.2 %collective-permute-start.18 = (bf16[2,2,128,128]{3,2,1,0:T(8,128)(2,1)S(1)}, bf16[2,2,128,128]{3,2,1,0:T(8,128)(2,1)S(1)}, u32[]{:S(2)}, u32[]{:S(2)}) collective-permute-start(bf16[2,2,128,128]{3,2,1,0:T(8,128)(2,1)S(1)} %copy.57), channel_id=1, source_target_pairs={{4,0},{8,4},{12,8},{16,12},{20,16},{24,20},{28,24},{5,1},{9,5},{13... | collective-permute-start | bytes 393224 | tf_op jit(solution)/shard_map/ppermute | solution.py:18
  127.3 9.7 %collective-permute-start.20 = (bf16[2,6,128,128]{3,2,1,0:T(8,128)(2,1)S(1)}, bf16[2,6,128,128]{3,2,1,0:T(8,128)(2,1)S(1)}, u32[]{:S(2)}, u32[]{:S(2)}) collective-permute-start(bf16[2,6,128,128]{3,2,1,0:T(8,128)(2,1)S(1)} %constant_dynamic-update-slice_fusion.6), channel_id=1, source_target_pairs={{1,0},{2,1},{3,2},{5,4},{6,5},{7,6},{9,8},{10,9},{11,10},{13,12},{... | collective-permute-start | bytes 1179656 | tf_op jit(solution)/shard_map/ppermute | solution.py:18
  129.8 8.3 %collective-permute-start.19 = (bf16[2,6,128,128]{3,2,1,0:T(8,128)(2,1)S(1)}, bf16[2,6,128,128]{3,2,1,0:T(8,128)(2,1)S(1)}, u32[]{:S(2)}, u32[]{:S(2)}) collective-permute-start(bf16[2,6,128,128]{3,2,1,0:T(8,128)(2,1)S(1)} %constant_dynamic-update-slice_fusion.6), channel_id=1, source_target_pairs={{0,1},{1,2},{2,3},{4,5},{5,6},{6,7},{8,9},{9,10},{10,11},{12,13},{... | collective-permute-start | bytes 1179656 | tf_op jit(solution)/shard_map/ppermute | solution.py:17
  150.0 3.8 %collective-permute-start.21 = (bf16[256,128]{1,0:T(8,128)(2,1)S(1)}, bf16[256,128]{1,0:T(8,128)(2,1)S(1)}, u32[]{:S(2)}, u32[]{:S(2)}) collective-permute-start(bf16[256,128]{1,0:T(8,128)(2,1)S(1)} %bitcast.97), channel_id=1, source_target_pairs={{0,1},{1,2},{2,3},{4,5},{5,6},{6,7},{8,9},{9,10},{10,11},{12,13},{... | collective-permute-start | bytes 196616 | tf_op jit(solution)/shard_map/ppermute | solution.py:26
